TPU v7x, 128 devices: a whole 4x4x4 slice. The times are simulated.
128 devices in a mesh: group: 32 (over y, z, core), context: 4 (over x).
Axes of the slice: x: 4, y: 4, z: 4, core: 2. Of those that a mesh axis runs over, the one named last changes fastest.
Arguments:
- inputs_load: bfloat16 [4, 32, 32, 24, 4096], P('context', 'group'), may hold values from -6 to 6
- maps_load: bfloat16 [4, 32, 32, 24, 256], P('context', 'group'), may hold values from -6 to 6
- steps_load: bfloat16 [4, 32, 32, 24, 64], P('context', 'group'), may hold values from 0 to 1, as said below
- decay_rate: float32 [64], replicated, may hold values from 1 to 4
- doc_lengths: int32 [32, 4], P('group'), may hold values from 1 to 2304, 3072 in all within a row
- forget_flags: int32 [32, 4], P('group'), may hold values 0 or 1
- out_grad: bfloat16 [32, 3072, 4096], P('group', 'context'), may hold values from -6 to 6
Outputs:
- layer_out: bfloat16 [32, 3072, 4096], P('group', 'context')
- grad_inputs: bfloat16 [4, 32, 32, 24, 4096], P('context', 'group')
- grad_maps: bfloat16 [4, 32, 32, 24, 256], P('context', 'group')
- grad_steps: bfloat16 [4, 32, 32, 24, 64], P('context', 'group')
Inputs may be any that keep to these rules, and one draw needn't show every extreme that they name: `doc_lengths`: each row sums to 3072; in every group one document has exactly 2304 positions. `steps_load`: positive step sizes.
All inputs are finite; a program needn't handle non-finite values. No bound on the sum of `forget_flags` on one device may be relied on, other than what follows from the above.
Results may differ from a plain program's by a relative error of at most 0.02.
Values may be sent and summed in bfloat16 or wider, within the bound.
A program may use at most 256 MiB of HBM per device.

v0:
```python
from functools import partial

import jax
import jax.numpy as jnp
from jax import lax
from jax.sharding import PartitionSpec as P

BLOCK = 256


def prefix(array, axis, join, neutral):
    place = lax.axis_index(axis)
    gathered = jax.tree.map(
        lambda a, kind: lax.all_gather(a.astype(kind), axis), array, (jnp.bfloat16, jnp.bfloat16)
    )
    state = jax.tree.map(lambda a, e: jnp.zeros_like(a) + jnp.asarray(e, a.dtype), array, neutral)

    def one(turn, state):
        return join(
            state,
            jax.tree.map(
                lambda a, own: lax.dynamic_index_in_dim(a, turn, 0, False).astype(own.dtype),
                gathered,
                array,
            ),
        )

    return lax.fori_loop(0, place, one, state)


def entering_2(array, axis, combine, identity):
    count, place = (lax.axis_size(axis), lax.axis_index(axis))
    everything = jax.tree.map(
        lambda part, kind: lax.all_gather(part.astype(kind), axis),
        array,
        jax.tree.map(lambda a: jnp.bfloat16 if a.dtype == jnp.float32 else a.dtype, array),
    )
    start = jax.tree.map(
        lambda part, zero: jnp.broadcast_to(jnp.asarray(zero, part.dtype), part.shape),
        array,
        identity,
    )

    def turn(k, before):
        at = count - 1 - k
        reached = at > place
        new = combine(
            before, jax.tree.map(lambda part, own: part[at].astype(own.dtype), everything, array)
        )
        return jax.tree.map(lambda a, b: jnp.where(reached, a, b), new, before)

    return lax.fori_loop(0, count, turn, start)


def segment_ids(lengths, positions):
    doc_ends = jnp.cumsum(lengths)
    return jnp.sum((positions[:, None] >= doc_ends[None, :]).astype(jnp.int32), axis=1)


def token_weight(segment, flag_row):
    doc_index = jnp.arange(flag_row.shape[0], dtype=jnp.int32)
    picked = jnp.sum(
        jnp.where(segment[:, None] == doc_index[None, :], flag_row[None, :], 0), axis=1
    )
    return 1.0 - 1.5 * picked.astype(jnp.float32)


def block_step(fading_factors, carried_in, pieces):
    old_state, previous = carried_in
    x_block, map_block, step_block, seg_block = pieces
    row_count = x_block.shape[0]
    head_count = fading_factors.shape[0]
    map_width = map_block.shape[1] // 2
    values = x_block.reshape(row_count, head_count, -1)
    b_part = map_block[:, :map_width].astype(jnp.bfloat16)
    c_part = map_block[:, map_width:].astype(jnp.bfloat16)
    cumulative = jnp.cumsum(-step_block * fading_factors[None, :], axis=0).T
    row_index = jnp.arange(row_count)
    kept_mask = (seg_block[:, None] == seg_block[None, :]) & (
        row_index[:, None] >= row_index[None, :]
    )
    spread = cumulative[:, :, None] - cumulative[:, None, :]
    decay_table = jnp.where(kept_mask[None], jnp.exp(jnp.where(kept_mask[None], spread, 0.0)), 0.0)
    scores = jnp.dot(c_part, b_part.T, preferred_element_type=jnp.float32)
    mixing = (decay_table * scores[None] * step_block.T[:, None, :]).astype(jnp.bfloat16)
    inner_out = jnp.einsum("hij,jhp->ihp", mixing, values, preferred_element_type=jnp.float32)
    opening = jnp.where((seg_block == previous)[None, :], jnp.exp(cumulative), 0.0)
    state_copy = old_state.astype(jnp.bfloat16)
    carried = (
        jnp.einsum("in,hpn->ihp", c_part, state_copy, preferred_element_type=jnp.float32)
        * opening.T[:, :, None]
    )
    last_seg = seg_block[row_count - 1]
    tail_weight = (
        jnp.where(
            (seg_block == last_seg)[None, :],
            jnp.exp(cumulative[:, row_count - 1 :] - cumulative),
            0.0,
        )
        * step_block.T
    )
    tail = (tail_weight.T[:, :, None] * values.astype(jnp.float32)).astype(jnp.bfloat16)
    fresh_state = jnp.einsum("jhp,jn->hpn", tail, b_part, preferred_element_type=jnp.float32)
    through = jnp.where(last_seg == previous, jnp.exp(cumulative[:, row_count - 1]), 0.0)
    new_state = fresh_state + through[:, None, None] * old_state
    return ((new_state, last_seg), (inner_out + carried).reshape(row_count, -1))


def run_blocks(
    values, map_rows, increment_line_entries, fading_factors, segment, first_state, previous
):
    row_count = values.shape[0]
    blocks = row_count // BLOCK
    pieces = (
        values.reshape(blocks, BLOCK, -1),
        map_rows.reshape(blocks, BLOCK, -1),
        increment_line_entries.reshape(blocks, BLOCK, -1),
        segment.reshape(blocks, BLOCK),
    )
    stepper = jax.checkpoint(partial(block_step, fading_factors))
    (final_state, last_seg), outputs = lax.scan(stepper, (first_state, previous), pieces)
    return (outputs.reshape(row_count, -1), final_state)


def chain(earlier, later):
    return (earlier[0] * later[0], later[1] + later[0][:, None, None] * earlier[1])


def through_decay(fading_factors, segment, previous, increment_line_entries):
    total_log = jnp.sum(-increment_line_entries * fading_factors[None, :], axis=0)
    return jnp.where(segment[segment.shape[0] - 1] == previous, jnp.exp(total_log), 0.0)


def correction(fading_factors, segment, previous, map_rows, increment_line_entries, entering):
    map_width = map_rows.shape[1] // 2
    row_count = map_rows.shape[0]
    blocks = row_count // BLOCK
    log_steps = (-increment_line_entries * fading_factors[None, :]).reshape(blocks, BLOCK, -1)
    block_totals = jnp.sum(log_steps, axis=1)
    before = jnp.cumsum(block_totals, axis=0) - block_totals
    cumulative = (jnp.cumsum(log_steps, axis=1) + before[:, None, :]).reshape(row_count, -1)
    opening = jnp.where((segment == previous)[:, None], jnp.exp(cumulative), 0.0)
    c_part = map_rows[:, map_width:].astype(jnp.bfloat16)
    reached = (
        jnp.einsum(
            "in,hpn->ihp", c_part, entering.astype(jnp.bfloat16), preferred_element_type=jnp.float32
        )
        * opening[:, :, None]
    )
    return reached.reshape(row_count, -1)


def on_device(inputs_load, maps_load, steps_load, decay_rate, doc_lengths, forget_flags, out_grad):
    head_count = decay_rate.shape[0]
    groups = lax.axis_size("group")
    piece_rows = inputs_load.shape[3]
    seq_dev = piece_rows * groups
    map_width = maps_load.shape[-1] // 2
    head_size = inputs_load.shape[-1] // head_count
    lengths = doc_lengths[0]
    flag_row = forget_flags[0]
    values, map_rows, increment_line_entries = (
        lax.all_to_all(inputs_load, "group", split_axis=2, concat_axis=1, tiled=True),
        lax.all_to_all(maps_load, "group", split_axis=2, concat_axis=1, tiled=True),
        lax.all_to_all(steps_load, "group", split_axis=2, concat_axis=1, tiled=True),
    )
    values = values.reshape(seq_dev, -1)
    map_rows = map_rows.reshape(seq_dev, -1).astype(jnp.float32)
    increment_line_entries = increment_line_entries.reshape(seq_dev, -1).astype(jnp.float32)
    offset = lax.axis_index("context") * seq_dev
    segment = segment_ids(lengths, offset + jnp.arange(seq_dev, dtype=jnp.int32))
    earlier_seg = segment_ids(lengths, jnp.reshape(offset - 1, (1,)))[0]
    previous = jnp.where(offset > 0, earlier_seg, -1)
    zero_state = jnp.zeros((head_count, head_size, map_width), jnp.float32)

    def forward(values, map_rows, increment_line_entries):
        return run_blocks(
            values, map_rows, increment_line_entries, decay_rate, segment, zero_state, previous
        )

    (local_out, local_state), pullback = jax.vjp(forward, values, map_rows, increment_line_entries)
    total_decay, decay_pull = jax.vjp(
        partial(through_decay, decay_rate, segment, previous), increment_line_entries
    )
    identity = (jnp.ones((head_count,), jnp.float32), zero_state)
    prefix_decay, entering = prefix((total_decay, local_state), "context", chain, identity)
    extra_out, extra_pull = jax.vjp(
        partial(correction, decay_rate, segment, previous),
        map_rows,
        increment_line_entries,
        entering,
    )
    layer_out = (local_out + extra_out).astype(jnp.bfloat16)
    weighted = out_grad[0].astype(jnp.float32) * token_weight(segment, flag_row)[:, None]
    extra_maps, extra_steps, direct = extra_pull(weighted)
    suffix_decay, leaving = entering_2((total_decay, direct), "context", chain, identity)
    (decay_steps,) = decay_pull(jnp.sum(leaving * entering, axis=(1, 2)))
    grad_values, grad_rows, grad_sizes = pullback((weighted, leaving))
    loader_shape = (1, groups, 1, piece_rows)
    grad_inputs, grad_maps, grad_steps = (
        lax.all_to_all(
            grad_values.reshape(loader_shape + (-1,)),
            "group",
            split_axis=1,
            concat_axis=2,
            tiled=True,
        ),
        lax.all_to_all(
            (grad_rows + extra_maps).astype(jnp.bfloat16).reshape(loader_shape + (-1,)),
            "group",
            split_axis=1,
            concat_axis=2,
            tiled=True,
        ),
        lax.all_to_all(
            (grad_sizes + extra_steps + decay_steps)
            .astype(jnp.bfloat16)
            .reshape(loader_shape + (-1,)),
            "group",
            split_axis=1,
            concat_axis=2,
            tiled=True,
        ),
    )
    return (layer_out[None], grad_inputs, grad_maps, grad_steps)


def solution(mesh):
    in_specs = (
        P("context", "group", None, None, None),
        P("context", "group", None, None, None),
        P("context", "group", None, None, None),
        P(),
        P("group", None),
        P("group", None),
        P("group", "context", None),
    )
    out_specs = (
        P("group", "context", None),
        P("context", "group", None, None, None),
        P("context", "group", None, None, None),
        P("context", "group", None, None, None),
    )
    return jax.shard_map(
        on_device, mesh=mesh, in_specs=in_specs, out_specs=out_specs, check_vma=False
    )
```

profile of v0, /device:TPU:15, one launch (start us, length us, event | category | flops | bytes accessed | tf_op | source)
XLA Modules:
  0.0 653.9 jit_solution(14328662785038460239)
XLA Ops:
  8.3 15.0 %all_to_all.63 = bf16[32,2,768]{2,1,0:T(2,128)(2,1)S(1)} all-to-all(bf16[32,2,768]{2,1,0:T(2,128)(2,1)S(1)} %reshape.715), channel_id=1, replica_groups=mesh['group'=32,'context'=4] {'group'}, dimensions={0} | all-to-all | bytes 196608 | tf_op jit(solution)/shard_map/all_to_all | solution.py:165
  23.3 14.9 %all_to_all.64 = bf16[1,1,32,24,256]{4,3,1,0,2:T(8,128)(2,1)} all-to-all(bf16[1,1,32,24,256]{4,3,1,0,2:T(8,128)(2,1)} %bitcast.458), channel_id=1, replica_groups=mesh['group'=32,'context'=4] {'group'}, dimensions={2} | all-to-all | bytes 786432 | tf_op jit(solution)/shard_map/all_to_all | solution.py:164
  45.0 9.4 %copy.198 = f32[1,768,4096]{1,2,0:T(8,128)} copy(bf16[1,768,4096]{2,1,0:T(8,128)(2,1)} %param.21) | data formatting | bytes 18874368 | tf_op jit(solution)/shard_map/convert_element_type | solution.py:194
  54.4 9.0 %convert_element_type.402 = f32[1,768,4096]{2,1,0:T(8,128)} convert(bf16[1,768,4096]{2,1,0:T(8,128)(2,1)} %param.21) | non-fusion elementwise | flops 3145728 | bytes 18874368 | tf_op jit(solution)/shard_map/convert_element_type | solution.py:194
  67.3 11.6 %broadcast_multiply_fusion = f32[3,256,4096]{2,1,0:T(8,128)} fusion(f32[3,256,4096]{2,1,0:T(8,128)} %bitcast.438, f32[3,256]{1,0:T(4,128)S(1)} %sub.151), kind=kLoop, calls=%fused_computation.170 | loop fusion | flops 3145728 | bytes 25168896 | tf_op jit(solution)/shard_map/mul | solution.py:194
  89.1 7.4 %fusion.118 = bf16[64,64,128]{2,1,0:T(8,128)(2,1)} fusion(f32[768,64,64]{0,2,1:T(8,128)} %bitcast.427, f32[768]{0:T(1024)S(1)} %multiply_subtract_fusion, f32[768,64]{0,1:T(8,128)S(1)} %broadcast_select_fusion.3, bf16[768,256]{1,0:T(8,128)(2,1)} %bitcast.48), kind=kOutput, calls=%fused_computation.176 | convolution fusion | flops 812122112 | bytes 14027776 | tf_op jit(solution)/shard_map/transpose(jvp(in,hpn->ihp))/dot_general | solution.py:145
  97.1 23.1 %all-to-all-done.1 = bf16[1,1,32,24,4096]{4,3,1,0,2:T(8,128)(2,1)} async-done(((bf16[1,1,32,24,4096]{4,3,1,0,2:T(8,128)(2,1)}), bf16[1,1,32,24,4096]{4,3,1,0,2:T(8,128)(2,1)}, u32[]{:S(2)}, u32[]{:S(2)}) %all-to-all-start.1) | async-done | bytes 6291488 | tf_op jit(solution)/shard_map/all_to_all | solution.py:163
  120.3 8.6 %copy.192 = bf16[3,256,4096]{1,2,0:T(8,128)(2,1)} copy(bf16[3,256,4096]{2,1,0:T(8,128)(2,1)} %bitcast.41) | data formatting | bytes 12582912
  128.9 98.5 %while.71 = (s32[]{:T(128)}, f32[64,64,128]{2,1,0:T(8,128)S(1)}, s32[]{:T(128)}, f32[3,256,4096]{2,1,0:T(8,128)}, f32[3,64,64,128]{3,2,1,0:T(8,128)}, /*index=5*...) while((s32[]{:T(128)}, f32[64,64,128]{2,1,0:T(8,128)S(1)}, ...), condition=%wide.region_6.7_spmd.clone, body=%wide.region_3.6_spmd.clone.sunk | while | flops 1125958400 | bytes 75574080 | solution.py:121
  143.9 6.8 %bitcast_add_fusion.6 = f32[256,64,64]{0,2,1:T(8,128)} fusion(f32[256,64,64]{0,2,1:T(8,128)S(1)} %copy-done.5, bf16[256,64,64]{0,2,1:T(8,128)(2,1)S(1)} %bitcast.433, f32[64,256]{1,0:T(8,128)S(1)} %get-tuple-element.1161, f32[256,256]{1,0:T(8,128)S(1)} %fusion.231, f32[64,256]{1,0:T(8,128)S(1)} %copy_bitcast_fusion.9, ...), kind=kOutput, calls=%fused_computation.119.clone.1 | convolution fusion | flops 564133888 | bytes 11010048 | tf_op jit(solution)/shard_map/jvp()/while/body/eval_jaxpr/hij,jhp->ihp/dot_general | solution.py:86
  176.7 6.8 %bitcast_add_fusion.6 = f32[256,64,64]{0,2,1:T(8,128)} fusion(f32[256,64,64]{0,2,1:T(8,128)S(1)} %copy-done.5, bf16[256,64,64]{0,2,1:T(8,128)(2,1)S(1)} %bitcast.433, f32[64,256]{1,0:T(8,128)S(1)} %get-tuple-element.1161, f32[256,256]{1,0:T(8,128)S(1)} %fusion.231, f32[64,256]{1,0:T(8,128)S(1)} %copy_bitcast_fusion.9, ...), kind=kOutput, calls=%fused_computation.119.clone.1 | convolution fusion | flops 564133888 | bytes 11010048 | tf_op jit(solution)/shard_map/jvp()/while/body/eval_jaxpr/hij,jhp->ihp/dot_general | solution.py:86
  228.7 13.6 %while.72 = (s32[]{:T(128)}, f32[64,64,128]{2,1,0:T(8,128)}, s32[]{:T(128)}, bf16[4,64,64,128]{3,2,1,0:T(8,128)(2,1)}, bf16[4,64]{1,0:T(4,128)(2,1)S(1)}, /*index=5*/s32[]{:T(128)}, s32[]{:T(128)}, s32[]{:T(128)}, s32[]{:T(128)}) while((s32[]{:T(128)}, f32[64,64,128]{2,1,0:T(8,128)}, s32[]{:T(128)}, ...), condition=%wide.region_16.17_spmd.clone, body=%wide.region_15.16_spmd.clone.sunk | while | flops 2621512 | bytes 5243695 | solution.py:52
  250.7 233.0 %while.70 = (s32[]{:T(128)}, f32[64,64,128]{2,1,0:T(8,128)}, bf16[3,256,4096]{2,1,0:T(8,128)(2,1)}, f32[3,256,256]{2,1,0:T(8,128)}, f32[3,256,64]{2,1,0:T(8,128)...) while((s32[]{:T(128)}, f32[64,64,128]{2,1,0:T(8,128)}, ...), condition=%wide.region_30.31_spmd, body=%wide.region_17.30_spmd.sunk | while | flops 2583479296 | bytes 136529840 | solution.py:121
  269.9 14.3 %fusion.214 = (f32[64,256]{1,0:T(8,128)S(1)}, f32[64,256]{1,0:T(8,128)S(1)}, f32[64,256]{1,0:T(8,128)}, bf16[256,256]{1,0:T(8,128)(2,1)S(1)}) fusion(f32[64,256]{1,0:T(8,128)S(1)} %copy.281, f32[256,256]{1,0:T(8,128)S(1)} %fusion.212, f32[64,256]{1,0:T(8,128)S(1)} %copy_bitcast_fusion.7, pred[256,256]{1,0:T(8,128)(4,1)S(1)} %fusion.213, ...), kind=kOutput, calls=%fused_computation.20.clone.1 | convolution fusion | flops 603865088 | bytes 7077888 | tf_op jit(solution)/shard_map/transpose(jvp())/while/body/eval_jaxpr/checkpoint/hij,jhp->ihp/dot_general | solution.py:86
  347.4 14.3 %fusion.214 = (f32[64,256]{1,0:T(8,128)S(1)}, f32[64,256]{1,0:T(8,128)S(1)}, f32[64,256]{1,0:T(8,128)}, bf16[256,256]{1,0:T(8,128)(2,1)S(1)}) fusion(f32[64,256]{1,0:T(8,128)S(1)} %copy.281, f32[256,256]{1,0:T(8,128)S(1)} %fusion.212, f32[64,256]{1,0:T(8,128)S(1)} %copy_bitcast_fusion.7, pred[256,256]{1,0:T(8,128)(4,1)S(1)} %fusion.213, ...), kind=kOutput, calls=%fused_computation.20.clone.1 | convolution fusion | flops 603865088 | bytes 7077888 | tf_op jit(solution)/shard_map/transpose(jvp())/while/body/eval_jaxpr/checkpoint/hij,jhp->ihp/dot_general | solution.py:86
  424.9 14.2 %fusion.214 = (f32[64,256]{1,0:T(8,128)S(1)}, f32[64,256]{1,0:T(8,128)S(1)}, f32[64,256]{1,0:T(8,128)}, bf16[256,256]{1,0:T(8,128)(2,1)S(1)}) fusion(f32[64,256]{1,0:T(8,128)S(1)} %copy.281, f32[256,256]{1,0:T(8,128)S(1)} %fusion.212, f32[64,256]{1,0:T(8,128)S(1)} %copy_bitcast_fusion.7, pred[256,256]{1,0:T(8,128)(4,1)S(1)} %fusion.213, ...), kind=kOutput, calls=%fused_computation.20.clone.1 | convolution fusion | flops 603865088 | bytes 7077888 | tf_op jit(solution)/shard_map/transpose(jvp())/while/body/eval_jaxpr/checkpoint/hij,jhp->ihp/dot_general | solution.py:86
  484.0 7.2 %while.69 = (s32[]{:T(128)}, f32[64,64,128]{2,1,0:T(8,128)S(1)}, s32[]{:T(128)}, bf16[4,64,64,128]{3,2,1,0:T(8,128)(2,1)}, bf16[4,64]{1,0:T(4,128)(2,1)}, /*index=5*/s32[]{:T(128)}, s32[]{:T(128)}, s32[]{:T(128)}) while((s32[]{:T(128)}, f32[64,64,128]{2,1,0:T(8,128)S(1)}, s32[]{:T(128)}, bf16[4,64,64,128]{3,2,1,0:T(8,128)(2,1)}, ...), condition=%wide.region_9.10_spmd, body=%wide.region_8.9_spmd.sunk | while | flops 1572933 | bytes 5243655 | solution.py:28
  491.2 8.7 %fusion.106 = (f32[768,64]{0,1:T(8,128)S(1)}, f32[768,64,64]{0,2,1:T(8,128)}) fusion(f32[768,64,64]{0,2,1:T(8,128)} %bitcast.428, f32[768]{0:T(1024)S(1)} %copy-done.22, f32[768,64]{0,1:T(8,128)S(1)} %copy-done.11, bf16[768,256]{1,0:T(8,128)(2,1)} %bitcast.48, f32[64,64,128]{2,1,0:T(8,128)S(1)} %get-tuple-element.603), kind=kOutput, calls=%fused_computation.161 | convolution fusion | flops 818364416 | bytes 27855872 | tf_op jit(solution)/shard_map/jvp(in,hpn->ihp)/dot_general | solution.py:145
  501.1 7.5 %reduce-window.86 = f32[3,64,2,128]{3,1,2,0:T(8,128)S(1)} reduce-window(f32[3,64,2,128]{3,1,2,0:T(8,128)S(1)} %bitcast.454, f32[]{:T(128)} %constant.200.clone.1), window={size=1x1x1x128 pad=0_0x0_0x0_0x0_127}, to_apply=%region_32.33 | reduce-window | flops 6242304 | bytes 393220 | tf_op jit(solution)/shard_map/reduce-window.7
  509.4 21.2 %all_to_all.65 = bf16[32,2,768]{2,1,0:T(2,128)(2,1)S(1)} all-to-all(bf16[32,2,768]{2,1,0:T(2,128)(2,1)S(1)} %reshape.717), channel_id=1, replica_groups=mesh['group'=32,'context'=4] {'group'}, dimensions={0} | all-to-all | bytes 196608 | tf_op jit(solution)/shard_map/all_to_all | solution.py:215
  536.6 12.6 %copy.197 = f32[1,768,4096]{2,1,0:T(8,128)} copy(f32[1,768,4096]{1,2,0:T(8,128)} %bitcast.437) | data formatting | bytes 25165824 | tf_op jit(solution)/shard_map/jvp()/reshape | solution.py:150
  556.6 56.3 %all-to-all-done.3 = bf16[1,32,1,24,4096]{4,3,2,0,1:T(8,128)(2,1)} async-done(((bf16[1,32,1,24,4096]{4,3,2,0,1:T(8,128)(2,1)}), bf16[1,32,1,24,4096]{4,3,2,0,1:T(8,128)(2,1)}, u32[]{:S(2)}, u32[]{:S(2)}) %all-to-all-start.3) | async-done | bytes 6291488 | tf_op jit(solution)/shard_map/all_to_all | solution.py:201
  612.8 14.3 %all-to-all-start.4 = ((bf16[1,32,1,24,256]{4,3,2,0,1:T(8,128)(2,1)}), bf16[1,32,1,24,256]{4,3,2,0,1:T(8,128)(2,1)S(1)}, u32[]{:S(2)}, u32[]{:S(2)}) async-start(bf16[1,32,1,24,256]{4,3,2,0,1:T(8,128)(2,1)} %bitcast.65), calls=%async_computation.4 | async-start | bytes 786432 | tf_op jit(solution)/shard_map/all_to_all | solution.py:208
  627.1 11.7 %fusion.107 = bf16[1,768,4096]{2,1,0:T(8,128)(2,1)} fusion(f32[1,768,4096]{2,1,0:T(8,128)} %copy.197, f32[1,768,4096]{2,1,0:T(8,128)} %bitcast.442), kind=kLoop, calls=%fused_computation.163 | loop fusion | flops 6291456 | bytes 31457280 | tf_op jit(solution)/shard_map/convert_element_type | solution.py:193
  (436 shorter events, 339.6 us)
Async XLA Ops:
  38.2 82.0 %all-to-all-start.1 = ((bf16[1,1,32,24,4096]{4,3,1,0,2:T(8,128)(2,1)}), bf16[1,1,32,24,4096]{4,3,1,0,2:T(8,128)(2,1)}, u32[]{:S(2)}, u32[]{:S(2)}) async-start(bf16[1,1,32,24,4096]{4,3,1,0,2:T(8,128)(2,1)} %bitcast.445), calls=%async_computation.1 | async-start | bytes 12582912 | tf_op jit(solution)/shard_map/all_to_all | solution.py:163
  44.0 184.7 %all-gather.8.cloned.1.call-start = ((), (), s32[]{:S(2)}) async-start(), calls=%async_computation.7 | async-start | bytes 5242880 | tf_op jit(solution)/shard_map/all_gather | solution.py:34
  54.4 10.9 %copy-start.31 = (s32[1,4]{1,0:T(1,128)S(1)}, s32[1,4]{1,0:T(1,128)}, u32[]{:S(2)}) copy-start(s32[1,4]{1,0:T(1,128)} %param.20) | copy-start | bytes 52
  54.4 11.1 %copy-start.36 = (u32[128]{0:T(128)S(1)}, u32[128]{0:T(128)}, u32[]{:S(2)}) copy-start(u32[128]{0:T(128)} %constant.225) | copy-start | bytes 1540
  65.4 23.7 %copy-start.21 = (f32[768]{0:T(1024)}, f32[768]{0:T(1024)S(1)}, u32[]{:S(2)}) copy-start(f32[768]{0:T(1024)S(1)} %multiply_subtract_fusion) | copy-start | bytes 9220
  67.2 12.0 %copy-start.23 = (f32[64]{0:T(128)S(1)}, f32[64]{0:T(128)}, u32[]{:S(2)}) copy-start(f32[64]{0:T(128)} %param.18) | copy-start | bytes 772
  80.1 16.5 %copy-start.26 = (f32[3,64]{1,0:T(4,128)}, f32[3,64]{1,0:T(4,128)S(1)}, u32[]{:S(2)}) copy-start(f32[3,64]{1,0:T(4,128)S(1)} %sub.148) | copy-start | bytes 2308
  82.3 14.3 %copy-start.24 = (f32[3,64,2]{1,2,0:T(2,128)}, f32[3,64,2]{1,2,0:T(2,128)S(1)}, u32[]{:S(2)}) copy-start(f32[3,64,2]{1,2,0:T(2,128)S(1)} %slice.155) | copy-start | bytes 4612
  82.6 14.0 %copy-start.29 = (f32[64]{0:T(128)}, f32[64]{0:T(128)S(1)}, u32[]{:S(2)}) copy-start(f32[64]{0:T(128)S(1)} %multiply_reduce_fusion.3) | copy-start | bytes 772
  89.1 7.5 %copy-start.10 = (f32[768,64]{0,1:T(8,128)}, f32[768,64]{0,1:T(8,128)S(1)}, u32[]{:S(2)}) copy-start(f32[768,64]{0,1:T(8,128)S(1)} %broadcast_select_fusion.3) | copy-start | bytes 589828
  96.6 387.1 %all-gather.6.cloned.1.call-start = ((), (), s32[]{:S(2)}) async-start(), calls=%async_computation.6 | async-start | bytes 5242880 | tf_op jit(solution)/shard_map/all_gather | solution.py:14
  268.5 15.6 %copy-start.16 = (f32[64,256]{1,0:T(8,128)}, f32[64,256]{1,0:T(8,128)S(1)}, u32[]{:S(2)}) copy-start(f32[64,256]{1,0:T(8,128)S(1)} %copy.281) | copy-start | bytes 196612 | tf_op jit(solution)/shard_map/transpose(jvp())/while
  268.7 15.4 %copy-start.8 = (f32[256,256]{1,0:T(8,128)}, f32[256,256]{1,0:T(8,128)S(1)}, u32[]{:S(2)}) copy-start(f32[256,256]{1,0:T(8,128)S(1)} %fusion.212) | copy-start | bytes 786436 | tf_op jit(solution)/shard_map/transpose(jvp())/while
  269.9 14.3 %copy-start.18 = (pred[256,256]{1,0:T(8,128)(4,1)}, pred[256,256]{1,0:T(8,128)(4,1)S(1)}, u32[]{:S(2)}) copy-start(pred[256,256]{1,0:T(8,128)(4,1)S(1)} %fusion.213) | copy-start | bytes 196612 | tf_op jit(solution)/shard_map/transpose(jvp())/while
  346.0 15.6 %copy-start.16 = (f32[64,256]{1,0:T(8,128)}, f32[64,256]{1,0:T(8,128)S(1)}, u32[]{:S(2)}) copy-start(f32[64,256]{1,0:T(8,128)S(1)} %copy.281) | copy-start | bytes 196612 | tf_op jit(solution)/shard_map/transpose(jvp())/while
  346.2 15.4 %copy-start.8 = (f32[256,256]{1,0:T(8,128)}, f32[256,256]{1,0:T(8,128)S(1)}, u32[]{:S(2)}) copy-start(f32[256,256]{1,0:T(8,128)S(1)} %fusion.212) | copy-start | bytes 786436 | tf_op jit(solution)/shard_map/transpose(jvp())/while
  347.4 14.3 %copy-start.18 = (pred[256,256]{1,0:T(8,128)(4,1)}, pred[256,256]{1,0:T(8,128)(4,1)S(1)}, u32[]{:S(2)}) copy-start(pred[256,256]{1,0:T(8,128)(4,1)S(1)} %fusion.213) | copy-start | bytes 196612 | tf_op jit(solution)/shard_map/transpose(jvp())/while
  423.5 15.6 %copy-start.16 = (f32[64,256]{1,0:T(8,128)}, f32[64,256]{1,0:T(8,128)S(1)}, u32[]{:S(2)}) copy-start(f32[64,256]{1,0:T(8,128)S(1)} %copy.281) | copy-start | bytes 196612 | tf_op jit(solution)/shard_map/transpose(jvp())/while
  423.7 15.4 %copy-start.8 = (f32[256,256]{1,0:T(8,128)}, f32[256,256]{1,0:T(8,128)S(1)}, u32[]{:S(2)}) copy-start(f32[256,256]{1,0:T(8,128)S(1)} %fusion.212) | copy-start | bytes 786436 | tf_op jit(solution)/shard_map/transpose(jvp())/while
  424.9 14.3 %copy-start.18 = (pred[256,256]{1,0:T(8,128)(4,1)}, pred[256,256]{1,0:T(8,128)(4,1)S(1)}, u32[]{:S(2)}) copy-start(pred[256,256]{1,0:T(8,128)(4,1)S(1)} %fusion.213) | copy-start | bytes 196612 | tf_op jit(solution)/shard_map/transpose(jvp())/while
  491.2 8.7 %copy-start.6 = (f32[64,64,128]{2,1,0:T(8,128)S(1)}, f32[64,64,128]{2,1,0:T(8,128)}, u32[]{:S(2)}) copy-start(f32[64,64,128]{2,1,0:T(8,128)} %get-tuple-element.1266) | copy-start | bytes 6291460
  499.9 9.3 %copy-start.20 = (f32[3,256,64]{2,1,0:T(8,128)S(1)}, f32[3,256,64]{2,1,0:T(8,128)}, u32[]{:S(2)}) copy-start(f32[3,256,64]{2,1,0:T(8,128)} %get-tuple-element.609) | copy-start | bytes 589828
  530.6 82.2 %all-to-all-start.3 = ((bf16[1,32,1,24,4096]{4,3,2,0,1:T(8,128)(2,1)}), bf16[1,32,1,24,4096]{4,3,2,0,1:T(8,128)(2,1)}, u32[]{:S(2)}, u32[]{:S(2)}) async-start(bf16[1,32,1,24,4096]{4,3,2,0,1:T(8,128)(2,1)} %bitcast.439), calls=%async_computation.3 | async-start | bytes 12582912 | tf_op jit(solution)/shard_map/all_to_all | solution.py:201
  612.8 26.9 %all-to-all-start.4 = ((bf16[1,32,1,24,256]{4,3,2,0,1:T(8,128)(2,1)}), bf16[1,32,1,24,256]{4,3,2,0,1:T(8,128)(2,1)S(1)}, u32[]{:S(2)}, u32[]{:S(2)}) async-start(bf16[1,32,1,24,256]{4,3,2,0,1:T(8,128)(2,1)} %bitcast.65), calls=%async_computation.4 | async-start | bytes 786432 | tf_op jit(solution)/shard_map/all_to_all | solution.py:208
  (46 other events, 206.8 us)
Sparse Core Ops, SparseCore 0:
  96.8 49.6 all-gather.7
  228.8 54.8 all-gather.5
where the time goes:
time: 663 us; the launch traced here: 654 us
  local copies, waits for them, and re-layouts  182 us (27%)
  matrix products  173 us (26%)
  other arithmetic  109 us (16%)
  waiting for transfers between devices  79.5 us (12%)
  blocking collectives  57.3 us (9%)
  starting transfers between devices  26.6 us (4%)
  between operations  16.7 us (3%)
  loops' own time  9.61 us (1%)
    dot_general x9, matrix products, block_step(): jnp.einsum('hij,jhp->ihp', mixing, values, preferred_element_type=jnp.flo...  83.6 us
    all_to_all x1, waiting for transfers between devices, on_device(): lax.all_to_all(grad_values.reshape(loader_shape + (-1,)), 'group', split_...  56.3 us
    dynamic_update_slice x15, local copies, waits for them, and re-layouts, run_blocks(): lax.scan(stepper, (first_state, previous), pieces)  53.3 us
    dynamic_slice x15, local copies, waits for them, and re-layouts, run_blocks(): lax.scan(stepper, (first_state, previous), pieces)  41.7 us
    dot_general x12, matrix products, block_step(): jnp.einsum('in,hpn->ihp', c_part, state_copy, preferred_element_type=jnp....  34.2 us
    dot_general x9, matrix products, block_step(): jnp.einsum('jhp,jn->hpn', tail, b_part, preferred_element_type=jnp.float32)  30.5 us
    all_to_all x1, waiting for transfers between devices, on_device(): lax.all_to_all(inputs_load, 'group', split_axis=2, concat_axis=1, tiled=T...  23.1 us
    dot_general x3, matrix products, correction(): jnp.einsum('in,hpn->ihp', c_part, entering.astype(jnp.bfloat16), preferre...  22.6 us
  transfers between devices with their start and end apart: 5, of which 2 were waited for; matrix products, arithmetic and copies ran while one was open for 66% of the time, Pallas kernels for 0%

commit v1 on v0

v1 whole, which is shorter than its diff:
```python
from functools import partial
from types import SimpleNamespace

import jax
import jax.numpy as jnp
from jax import lax
from jax.experimental import pallas as pl
from jax.experimental.pallas import tpu as pltpu
from jax.sharding import PartitionSpec as P

BLOCK = 128
CHUNK_HEADS = 8
AHEAD = 3
LANES = 128
LOG2E = 1.4426950408889634
MESH = pl.DeviceIdType.MESH
F32 = jnp.float32
BF16 = jnp.bfloat16


def dot_nn(a, b):
    return jnp.dot(a, b, preferred_element_type=F32)


def dot_nt(a, b):
    return lax.dot_general(a, b, (((1,), (1,)), ((), ())), preferred_element_type=F32)


def dot_tn(a, b):
    return lax.dot_general(a, b, (((0,), (0,)), ((), ())), preferred_element_type=F32)


def dot_exact(a, b):
    return jnp.dot(a, b, precision=lax.Precision.HIGHEST, preferred_element_type=F32)


def halves(a):
    high = a.astype(BF16)
    return jnp.concatenate([high, (a - high.astype(F32)).astype(BF16)], axis=1)


def loop(count, body):
    def step(i, carry):
        body(i)
        return carry

    lax.fori_loop(0, count, step, 0)


def kernel(dims, names, *refs):
    r = SimpleNamespace(**dict(zip(names, refs)))
    groups, slices, piece, heads, size = dims
    seq = groups * piece
    blocks = seq // BLOCK
    chunks = heads // CHUNK_HEADS
    width = CHUNK_HEADS * size
    docs = r.lens.shape[1]
    me, place = lax.axis_index("group"), lax.axis_index("context")
    offset = place * seq

    def peer(i):
        return lax.rem(me + i, groups)

    def ctx(i):
        return lax.rem(place + i, slices)

    def rows(b):
        return pl.ds(pl.multiple_of(b * BLOCK, BLOCK), BLOCK)

    def cols(k):
        return pl.ds(pl.multiple_of(k * width, width), width)

    def piece_rows(j):
        return pl.ds(pl.multiple_of(j * piece, 8), piece)

    def to_group(src, dst, send, recv, j):
        return pltpu.make_async_remote_copy(
            src_ref=src, dst_ref=dst, send_sem=send, recv_sem=recv,
            device_id={"group": j}, device_id_type=MESH,
        )

    def to_context(src, dst, send, recv, c):
        return pltpu.make_async_remote_copy(
            src_ref=src, dst_ref=dst, send_sem=send, recv_sem=recv,
            device_id={"context": c}, device_id_type=MESH,
        )

    def take(ref, sem):
        pltpu.make_async_copy(ref, ref, sem).wait()

    barrier = pltpu.get_barrier_semaphore()

    def greet_group(i):
        pl.semaphore_signal(barrier, inc=1, device_id={"group": peer(i + 1)}, device_id_type=MESH)

    def greet_context(i):
        pl.semaphore_signal(barrier, inc=1, device_id={"context": ctx(i + 1)}, device_id_type=MESH)

    loop(groups - 1, greet_group)
    loop(slices - 1, greet_context)
    pl.semaphore_wait(barrier, groups + slices - 2)

    def send_side(i):
        j = peer(i + 1)
        to_group(r.side_hbm.at[j], r.side.at[me], r.side_send.at[0], r.side_recv.at[0], j).start()

    def own_side():
        return pltpu.make_async_copy(r.side_hbm.at[me], r.side.at[me], r.side_own.at[0])

    def send_values(k):
        def one(i):
            j = peer(i + 1)
            to_group(
                r.x_hbm.at[j, :, cols(k)], r.vals.at[k, me], r.val_send.at[k], r.val_recv.at[k], j
            ).start()

        loop(groups - 1, one)
        own_values(k).start()

    def own_values(k):
        return pltpu.make_async_copy(
            r.x_hbm.at[me, :, cols(k)], r.vals.at[k, me], r.val_own.at[k]
        )

    def load_grad(k):
        slot = lax.rem(k, 3)
        return pltpu.make_async_copy(r.og_hbm.at[:, cols(k)], r.og.at[slot], r.og_sem.at[slot])

    def store_out(k):
        slot = lax.rem(k, 2)
        return pltpu.make_async_copy(r.y.at[slot], r.y_hbm.at[:, cols(k)], r.y_sem.at[slot])

    loop(groups - 1, send_side)
    own_side().start()
    loop(min(AHEAD, chunks), send_values)
    load_grad(0).start()

    take(r.side.at[pl.ds(0, groups - 1)], r.side_recv.at[0])
    own_side().wait()

    def unpack_side(j):
        r.sidef[piece_rows(j), :] = r.side[j].astype(F32)

    loop(groups, unpack_side)

    ends = [r.lens[0, 0]]
    for d in range(1, docs):
        ends.append(ends[-1] + r.lens[0, d])

    def segment(position):
        return sum(jnp.where(position >= end, 1, 0) for end in ends)

    row_at = lax.broadcasted_iota(jnp.int32, (BLOCK, BLOCK), 0)
    col_at = lax.broadcasted_iota(jnp.int32, (BLOCK, BLOCK), 1)
    rate = r.rate[0:1, :]

    def block_segments(b):
        first = offset + b * BLOCK
        before = jnp.where(first > 0, segment(first - 1), -1)
        last = segment(first + BLOCK - 1)
        return segment(first + row_at), segment(first + col_at), before, last

    def prepare(b):
        seg_row, seg_col, before, last = block_segments(b)
        kept = (seg_row == seg_col) & (row_at >= col_at)
        r.mask[b] = jnp.where(kept, 0.0, -1e30)
        part = r.sidef[rows(b), :]
        b_map, c_map, step = part[:, :LANES], part[:, LANES : 2 * LANES], part[:, 2 * LANES :]
        b_part, c_part = b_map.astype(BF16), c_map.astype(BF16)
        r.b_map[b], r.c_map[b] = b_part, c_part
        r.b_turned[b], r.c_turned[b] = b_map.T.astype(BF16), c_map.T.astype(BF16)
        r.scores[b] = dot_nt(c_part, b_part)
        r.step[b] = step.astype(BF16)
        lower = jnp.where(row_at >= col_at, 1.0, 0.0)
        cum = dot_exact(lower, step * (rate * -LOG2E))
        end = cum[BLOCK - 1 : BLOCK, :]
        r.opening[b] = halves(jnp.where(seg_row == before, jnp.exp2(cum), 0.0))
        r.tail[b] = halves(jnp.where(seg_row == last, jnp.exp2(end - cum), 0.0))
        r.through[pl.ds(b, 1), :] = jnp.where(last == before, jnp.exp2(end), 0.0)
        for k in range(chunks):
            r.cum_col[b, k] = cum[:, k * CHUNK_HEADS : (k + 1) * CHUNK_HEADS]
        r.cum_row[b] = cum.T
        picked = sum(jnp.where(seg_row == d, r.flags[0, d], 0) for d in range(docs))
        r.weight[b] = 1.0 - 1.5 * picked.astype(F32)
        r.dscores[b] = jnp.zeros((BLOCK, BLOCK), F32)
        for name in ("dc", "db", "edge", "dstep"):
            getattr(r, name)[b] = jnp.zeros((BLOCK, LANES), F32)

    r.through[...] = jnp.ones(r.through.shape, F32)
    r.flow[...] = jnp.zeros(r.flow.shape, F32)
    loop(blocks, prepare)

    decay = r.through[0:1, :]
    for b in range(1, blocks):
        decay = decay * r.through[b : b + 1, :]
    r.decay_own[...] = jnp.broadcast_to(decay, r.decay_own.shape)

    def send_decay(i):
        c = ctx(i + 1)
        to_context(
            r.decay_own, r.decays.at[place], r.decay_send.at[0], r.decay_recv.at[0], c
        ).start()

    loop(slices - 1, send_decay)
    take(r.decays.at[pl.ds(0, slices - 1)], r.decay_recv.at[0])
    take(r.decays.at[pl.ds(0, slices - 1)], r.decay_send.at[0])

    def spread(k):
        head = lax.broadcasted_iota(jnp.int32, (LANES, width), 0)
        col = lax.broadcasted_iota(jnp.int32, (LANES, width), 1)
        low = (head - k * CHUNK_HEADS) * size
        return jnp.where((col >= low) & (col < low + size), 1.0, 0.0).astype(BF16)

    def first_half(k):
        slot, held = lax.rem(k, 2), lax.rem(k, 3)
        take(r.vals.at[k, pl.ds(0, groups - 1)], r.val_recv.at[k])
        own_values(k).wait()
        load_grad(k).wait()

        def unpack(j):
            r.x[slot, piece_rows(j), :] = r.vals[k, j].astype(F32)

        loop(groups, unpack)
        one = spread(k)
        r.one[slot, pl.ds(0, LANES)] = one
        r.one[slot, pl.ds(LANES, LANES)] = one
        r.through_wide[slot] = dot_nn(halves(r.through[...]), r.one[slot])
        r.run[...] = jnp.zeros(r.run.shape, F32)

        def fresh(b):
            both = r.one[slot]
            step = dot_nn(r.step[b], both[:LANES])
            tail = dot_nn(r.tail[b], both)
            scaled = (r.x[slot, rows(b), :] * step * tail).astype(BF16)
            r.fresh[slot, b] = dot_nn(r.b_turned[b], scaled)
            through = r.through_wide[slot, pl.ds(b, 1), :]
            r.run[...] = through * r.run[...] + r.fresh[slot, b]
            opening = dot_nn(r.opening[b], both)
            grad = r.og[held, rows(b), :].astype(F32) * r.weight[b][:, :1]
            r.og[held, rows(b), :] = grad.astype(BF16)
            r.dfresh[slot, b] = dot_nn(r.c_turned[b], (grad * opening).astype(BF16))

        loop(blocks, fresh)
        r.states[k, 0] = r.run[...].astype(BF16)
        r.run[...] = jnp.zeros(r.run.shape, F32)

        def back(turn):
            b = blocks - 1 - turn
            through = r.through_wide[slot, pl.ds(b, 1), :]
            r.run[...] = through * r.run[...] + r.dfresh[slot, b]

        loop(blocks, back)
        r.states[k, 1] = r.run[...].astype(BF16)

        def send_state(i):
            c = ctx(i + 1)
            kind = jnp.where(c > place, 0, 1)
            to_context(
                r.states.at[k, kind], r.around.at[k, place], r.state_send.at[k], r.state_recv.at[k], c
            ).start()

        loop(slices - 1, send_state)

    def second_half(k):
        slot, held = lax.rem(k, 2), lax.rem(k, 3)
        take(r.around.at[k, pl.ds(0, slices - 1)], r.state_recv.at[k])

        def widened(c):
            return dot_nn(halves(r.decays[c]), r.one[slot])[:1]

        r.run[...] = jnp.zeros(r.run.shape, F32)

        def enter(c):
            @pl.when(c < place)
            def _():
                r.run[...] = r.around[k, c].astype(F32) + widened(c) * r.run[...]

        loop(slices, enter)

        def forward(b):
            r.state[b] = r.run[...].astype(BF16)
            through = r.through_wide[slot, pl.ds(b, 1), :]
            new = through * r.run[...] + r.fresh[slot, b]
            r.run[...] = new
            r.fresh[slot, b] = new

        loop(blocks, forward)
        r.run[...] = jnp.zeros(r.run.shape, F32)

        def leave(turn):
            c = slices - 1 - turn

            @pl.when(c > place)
            def _():
                r.run[...] = r.around[k, c].astype(F32) + widened(c) * r.run[...]

        loop(slices, leave)
        r.flow_wide[...] = jnp.zeros(r.flow_wide.shape, F32)

        def backward(turn):
            b = blocks - 1 - turn
            now = r.run[...]
            r.dstate[b] = now.astype(BF16)
            r.flow_wide[pl.ds(b, 1), :] = jnp.sum(now * r.fresh[slot, b], axis=0, keepdims=True)
            through = r.through_wide[slot, pl.ds(b, 1), :]
            r.run[...] = through * now + r.dfresh[slot, b]

        loop(blocks, backward)
        one = r.one[slot, pl.ds(0, LANES)]

        def per_head(a):
            high = a.astype(BF16)
            low = (a - high.astype(F32)).astype(BF16)
            return dot_nt(high, one) + dot_nt(low, one)

        r.flow[...] += per_head(r.flow_wide[...])

        @pl.when(k >= 2)
        def _():
            store_out(k - 2).wait()

        lane = lax.broadcasted_iota(jnp.int32, (1, LANES), 1)
        left = jnp.where(lane < size, 1.0, 0.0).astype(BF16)
        right = jnp.where(lane < size, 0.0, 1.0).astype(BF16)

        def block(b):
            both = r.one[slot]
            x = r.x[slot, rows(b), :]
            step = dot_nn(r.step[b], both[:LANES])
            tail = dot_nn(r.tail[b], both)
            opening = dot_nn(r.opening[b], both)
            grad = r.og[held, rows(b), :]
            stepped = x * step
            xd = stepped.astype(BF16)
            state, dstate = r.state[b], r.dstate[b]
            carried = dot_nn(r.c_map[b], state) * opening
            r.dc[b] += dot_nt((grad.astype(F32) * opening).astype(BF16), state)
            r.db[b] += dot_nt((stepped * tail).astype(BF16), dstate)
            dtail = dot_nn(r.b_map[b], dstate) * tail
            mask, scores = r.mask[b], r.scores[b]
            cum_row = r.cum_row[b, pl.ds(pl.multiple_of(k * CHUNK_HEADS, 8), CHUNK_HEADS), :]
            cum_col = r.cum_col[b, k]
            dscores = r.dscores[b]
            ys, dxs = [], []
            for p in range(width // LANES):
                at = slice(p * LANES, (p + 1) * LANES)
                xp, gp = xd[:, at], grad[:, at]
                x_two = jnp.concatenate([xp * left, xp * right], axis=0)
                g_two = jnp.concatenate([gp * left, gp * right], axis=0)
                dmixing = dot_nt(gp, x_two)
                mixing = []
                for q in range(2):
                    h = 2 * p + q
                    fade = jnp.exp2(cum_col[:, h : h + 1] - cum_row[h : h + 1, :] + mask)
                    mixing.append((fade * scores).astype(BF16))
                    dscores = dscores + dmixing[:, q * BLOCK : (q + 1) * BLOCK] * fade
                ys.append(dot_nn(jnp.concatenate(mixing, axis=1), x_two))
                dxs.append(dot_tn(jnp.concatenate(mixing, axis=0), g_two))
            r.dscores[b] = dscores
            y = jnp.concatenate(ys, axis=1) + carried
            dxd = jnp.concatenate(dxs, axis=1) + dtail
            r.y[slot, rows(b), :] = y.astype(BF16)
            r.gx[rows(b), :] = dxd * step
            r.edge[b] += per_head(grad.astype(F32) * y - xd.astype(F32) * dxd)
            r.dstep[b] += per_head(x * dxd)

        loop(blocks, block)
        store_out(k).start()

        def give(i):
            j = peer(i)
            r.gsend[k, j] = r.gx[piece_rows(j), :].astype(BF16)

            @pl.when(i > 0)
            def _():
                to_group(
                    r.gsend.at[k, j], r.gx_hbm.at[me, :, cols(k)], r.gx_send.at[k], r.gx_recv.at[k], j
                ).start()

        loop(groups, give)
        own_gradient(k).start()

    def own_gradient(k):
        return pltpu.make_async_copy(
            r.gsend.at[k, me], r.gx_hbm.at[me, :, cols(k)], r.gx_own.at[k]
        )

    def turn(k):
        @pl.when(k + AHEAD < chunks)
        def _():
            send_values(k + AHEAD)

        @pl.when(k < chunks)
        def _():
            @pl.when(k + 1 < chunks)
            def _():
                load_grad(k + 1).start()

            first_half(k)

        @pl.when(k > 0)
        def _():
            second_half(k - 1)

    loop(chunks + 1, turn)

    def finish(b):
        seg_row, seg_col, before, last = block_segments(b)
        dscores = r.dscores[b].astype(BF16)
        later = jnp.where((seg_row == seg_col) & (col_at >= row_at), 1.0, 0.0)
        dlog = dot_exact(later, r.edge[b])
        dlog = dlog + jnp.where(seg_row == last, r.flow[pl.ds(b, 1), :], 0.0)
        r.sidef[rows(b), pl.ds(0, LANES)] = r.db[b] + dot_tn(dscores, r.c_map[b])
        r.sidef[rows(b), pl.ds(LANES, LANES)] = r.dc[b] + dot_nn(dscores, r.b_map[b])
        r.sidef[rows(b), pl.ds(2 * LANES, LANES)] = r.dstep[b] - rate * dlog

    loop(blocks, finish)

    def give_side(i):
        j = peer(i)
        r.gside[j] = r.sidef[piece_rows(j), :].astype(BF16)

        @pl.when(i > 0)
        def _():
            to_group(
                r.gside.at[j], r.gside_hbm.at[me], r.gside_send.at[0], r.gside_recv.at[0], j
            ).start()

    loop(groups, give_side)
    own = pltpu.make_async_copy(r.gside.at[me], r.gside_hbm.at[me], r.gside_own.at[0])
    own.start()

    def settle(k):
        take(r.vals.at[k, pl.ds(0, groups - 1)], r.val_send.at[k])
        take(r.around.at[k, pl.ds(0, slices - 1)], r.state_send.at[k])
        take(r.vals.at[k, pl.ds(0, groups - 1)], r.gx_send.at[k])
        take(r.vals.at[k, pl.ds(0, groups - 1)], r.gx_recv.at[k])
        own_gradient(k).wait()

    loop(chunks, settle)
    for k in range(max(chunks - 2, 0), chunks):
        store_out(k).wait()
    own.wait()
    for sem in (r.side_send, r.gside_send, r.gside_recv):
        take(r.side.at[pl.ds(0, groups - 1)], sem.at[0])


def on_device(inputs_load, maps_load, steps_load, decay_rate, doc_lengths, forget_flags, out_grad):
    groups, slices = lax.axis_size("group"), lax.axis_size("context")
    heads = decay_rate.shape[0]
    piece, total = inputs_load.shape[3:]
    size = total // heads
    seq = groups * piece
    blocks = seq // BLOCK
    chunks = heads // CHUNK_HEADS
    width = CHUNK_HEADS * size
    fill = LANES - heads
    side = jnp.concatenate(
        [maps_load, steps_load, jnp.zeros(steps_load.shape[:-1] + (fill,), BF16)], axis=-1
    ).reshape(groups, piece, 3 * LANES)
    rate = jnp.broadcast_to(jnp.pad(decay_rate, (0, fill))[None], (8, LANES))

    dma = pltpu.SemaphoreType.DMA
    vmem = pltpu.VMEM
    scratch = dict(
        vals=vmem((chunks, groups, piece, width), BF16),
        gsend=vmem((chunks, groups, piece, width), BF16),
        side=vmem((groups, piece, 3 * LANES), BF16),
        gside=vmem((groups, piece, 3 * LANES), BF16),
        sidef=vmem((seq, 3 * LANES), F32),
        og=vmem((3, seq, width), BF16),
        y=vmem((2, seq, width), BF16),
        x=vmem((2, seq, width), F32),
        gx=vmem((seq, width), F32),
        one=vmem((2, 2 * LANES, width), BF16),
        fresh=vmem((2, blocks, LANES, width), F32),
        dfresh=vmem((2, blocks, LANES, width), F32),
        state=vmem((blocks, LANES, width), BF16),
        dstate=vmem((blocks, LANES, width), BF16),
        run=vmem((LANES, width), F32),
        states=vmem((chunks, 2, LANES, width), BF16),
        around=vmem((chunks, slices, LANES, width), BF16),
        decays=vmem((slices, 8, LANES), F32),
        decay_own=vmem((8, LANES), F32),
        through=vmem((8, LANES), F32),
        through_wide=vmem((2, 8, width), F32),
        flow=vmem((8, LANES), F32),
        flow_wide=vmem((8, width), F32),
        mask=vmem((blocks, BLOCK, BLOCK), F32),
        scores=vmem((blocks, BLOCK, BLOCK), F32),
        dscores=vmem((blocks, BLOCK, BLOCK), F32),
        weight=vmem((blocks, BLOCK, BLOCK), F32),
        b_map=vmem((blocks, BLOCK, LANES), BF16),
        c_map=vmem((blocks, BLOCK, LANES), BF16),
        b_turned=vmem((blocks, LANES, BLOCK), BF16),
        c_turned=vmem((blocks, LANES, BLOCK), BF16),
        step=vmem((blocks, BLOCK, LANES), BF16),
        opening=vmem((blocks, BLOCK, 2 * LANES), BF16),
        tail=vmem((blocks, BLOCK, 2 * LANES), BF16),
        cum_col=vmem((blocks, chunks, BLOCK, CHUNK_HEADS), F32),
        cum_row=vmem((blocks, LANES, BLOCK), F32),
        dc=vmem((blocks, BLOCK, LANES), F32),
        db=vmem((blocks, BLOCK, LANES), F32),
        edge=vmem((blocks, BLOCK, LANES), F32),
        dstep=vmem((blocks, BLOCK, LANES), F32),
        side_send=dma((1,)), side_recv=dma((1,)), side_own=dma((1,)),
        gside_send=dma((1,)), gside_recv=dma((1,)), gside_own=dma((1,)),
        decay_send=dma((1,)), decay_recv=dma((1,)),
        val_send=dma((chunks,)), val_recv=dma((chunks,)), val_own=dma((chunks,)),
        gx_send=dma((chunks,)), gx_recv=dma((chunks,)), gx_own=dma((chunks,)),
        state_send=dma((chunks,)), state_recv=dma((chunks,)),
        og_sem=dma((3,)), y_sem=dma((2,)),
    )
    names = (
        "x_hbm", "side_hbm", "og_hbm", "rate", "lens", "flags", "y_hbm", "gx_hbm", "gside_hbm",
    ) + tuple(scratch)
    anywhere = pl.BlockSpec(memory_space=pl.ANY)
    in_vmem = pl.BlockSpec(memory_space=pltpu.VMEM)
    in_smem = pl.BlockSpec(memory_space=pltpu.SMEM)
    y, gx, gside = pl.pallas_call(
        partial(kernel, (groups, slices, piece, heads, size), names),
        out_shape=(
            jax.ShapeDtypeStruct((seq, total), BF16),
            jax.ShapeDtypeStruct((groups, piece, total), BF16),
            jax.ShapeDtypeStruct((groups, piece, 3 * LANES), BF16),
        ),
        in_specs=[anywhere, anywhere, anywhere, in_vmem, in_smem, in_smem],
        out_specs=[anywhere, anywhere, anywhere],
        scratch_shapes=list(scratch.values()),
        compiler_params=pltpu.CompilerParams(
            collective_id=0, has_side_effects=True, vmem_limit_bytes=60 * 1024 * 1024
        ),
        name="layer",
    )(
        inputs_load.reshape(groups, piece, total), side, out_grad[0], rate, doc_lengths, forget_flags
    )
    gside = gside[None, None]
    return (
        y[None],
        gx[None, None],
        gside[..., : 2 * LANES],
        gside[..., 2 * LANES : 2 * LANES + heads],
    )


def solution(mesh):
    in_specs = (
        P("context", "group", None, None, None),
        P("context", "group", None, None, None),
        P("context", "group", None, None, None),
        P(),
        P("group", None),
        P("group", None),
        P("group", "context", None),
    )
    out_specs = (
        P("group", "context", None),
        P("context", "group", None, None, None),
        P("context", "group", None, None, None),
        P("context", "group", None, None, None),
    )
    return jax.shard_map(
        on_device, mesh=mesh, in_specs=in_specs, out_specs=out_specs, check_vma=False
    )
```

time: 663 us -> 212 us (0.32)
  the two profiles are of different devices: /device:TPU:15 before, /device:TPU:1 now
where the time goes in v1:
time: 212 us
  Pallas kernels  195 us (92%)
  local copies, waits for them, and re-layouts  14 us (7%)
    pallas_call x1, Pallas kernels, on_device(): pl.pallas_call(partial(kernel, (groups, slices, piece, heads, size), name...  195 us
    unnamed x6, local copies, waits for them, and re-layouts  9.14 us

profile of v1, /device:TPU:1, one launch (start us, length us, event | category | flops | bytes accessed | tf_op | source)
XLA Modules:
  0.0 211.6 jit_solution(12608021904115262018)
XLA Ops:
  0.6 0.7 pad.4
  1.3 0.1 pad.7.clone
  1.4 0.6 broadcast_in_dim.19.refs_3_
  2.0 2.0 maximum_bitcast_fusion.refs_1_
  4.0 194.9 %layer.1 = (bf16[768,4096]{1,0:T(8,128)(2,1)}, bf16[32,24,4096]{2,1,0:T(8,128)(2,1)}, bf16[32,24,384]{2,1,0:T(8,128)(2,1)}) custom-call(bf16[32,24,4096]{2,1,0:T(8,128)(2,1)} %bitcast.7, bf16[32,24,384]{2,1,0:T(8,128)(2,1)} %maximum_bitcast_fusion.refs_1_, bf16[768,4096]{1,0:T(8,128)(2,1)} %bitcast.8, f32[8,128]{1,0:T(8,128)} %broadcast_in_dim.19.refs_3_, ...), custom_call_target="tpu_custom_call" | custom-call | tf_op jit(solution)/shard_map/layer/pallas_call | solution.py:520
  198.9 1.6 slice.9
  200.5 0.0 slice-start
  200.5 1.9 slice.8
  202.4 0.0 slice-start.1
  202.4 6.4 %copy.13 = bf16[1,768,4096]{2,1,0:T(8,128)(2,1)} copy(bf16[1,768,4096]{2,1,0:T(8,128)(2,1)} %bitcast.12) | data formatting | bytes 12582912
  208.9 0.0 slice-done
  208.9 0.0 slice-done.1
  208.9 2.7 %copy.14 = bf16[1,1,32,24,4096]{4,3,2,1,0:T(8,128)(2,1)} copy(bf16[1,1,32,24,4096]{4,3,2,1,0:T(8,128)(2,1)S(1)} %bitcast.11) | data formatting | bytes 12582912
  (2 shorter events, 0.0 us)
Async XLA Ops:
  200.5 8.4 %slice-start = ((s8[6291456]{0:T(1024)(128)(4,1)}), s8[4194304]{0:T(1024)(128)(4,1)S(1)}, s32[]{:S(2)}) async-start(s8[6291456]{0:T(1024)(128)(4,1)} %bitcast.9), calls=%async_computation | async-start | bytes 8388608
  202.4 6.4 %slice-start.1 = ((s8[6291456]{0:T(1024)(128)(4,1)}), s8[2097152]{0:T(1024)(128)(4,1)S(1)}, s32[]{:S(2)}) async-start(s8[6291456]{0:T(1024)(128)(4,1)} %bitcast.9), calls=%async_computation.1 | async-start | bytes 4194304

commit v2 on v1

--- a/solution.py
+++ b/solution.py
@@ -61,6 +61,20 @@
     def peer(i):
         return lax.rem(me + i, groups)
 
+    turns = ((0, 1), (1, 0), (0, 3), (3, 0), (0, 2), (2, 0), (1, 1), (3, 3), (1, 3), (3, 1))
+    turns += ((2, 2), (1, 2), (2, 1), (3, 2), (2, 3))
+
+    def others():
+        if groups != 32:
+            return [peer(i) for i in range(1, groups)]
+        core, z, y = lax.rem(me, 2), lax.rem(me // 2, 4), me // 8
+        found = []
+        for other in (0, 1):
+            for dy, dz in turns:
+                chip = lax.rem(y + dy, 4) * 4 + lax.rem(z + dz, 4)
+                found.append(chip * 2 + lax.rem(core + other, 2))
+        return found + [me + 1 - 2 * core]
+
     def ctx(i):
         return lax.rem(place + i, slices)
 
@@ -100,21 +114,17 @@
     loop(slices - 1, greet_context)
     pl.semaphore_wait(barrier, groups + slices - 2)
 
-    def send_side(i):
-        j = peer(i + 1)
+    def send_side(j):
         to_group(r.side_hbm.at[j], r.side.at[me], r.side_send.at[0], r.side_recv.at[0], j).start()
 
     def own_side():
         return pltpu.make_async_copy(r.side_hbm.at[me], r.side.at[me], r.side_own.at[0])
 
     def send_values(k):
-        def one(i):
-            j = peer(i + 1)
+        for j in others():
             to_group(
                 r.x_hbm.at[j, :, cols(k)], r.vals.at[k, me], r.val_send.at[k], r.val_recv.at[k], j
             ).start()
-
-        loop(groups - 1, one)
         own_values(k).start()
 
     def own_values(k):
@@ -130,7 +140,8 @@
         slot = lax.rem(k, 2)
         return pltpu.make_async_copy(r.y.at[slot], r.y_hbm.at[:, cols(k)], r.y_sem.at[slot])
 
-    loop(groups - 1, send_side)
+    for j in others():
+        send_side(j)
     own_side().start()
     loop(min(AHEAD, chunks), send_values)
     load_grad(0).start()
@@ -367,17 +378,15 @@
         loop(blocks, block)
         store_out(k).start()
 
-        def give(i):
-            j = peer(i)
+        def pack(j):
             r.gsend[k, j] = r.gx[piece_rows(j), :].astype(BF16)
 
-            @pl.when(i > 0)
-            def _():
-                to_group(
-                    r.gsend.at[k, j], r.gx_hbm.at[me, :, cols(k)], r.gx_send.at[k], r.gx_recv.at[k], j
-                ).start()
-
-        loop(groups, give)
+        for j in others():
+            pack(j)
+            to_group(
+                r.gsend.at[k, j], r.gx_hbm.at[me, :, cols(k)], r.gx_send.at[k], r.gx_recv.at[k], j
+            ).start()
+        pack(me)
         own_gradient(k).start()
 
     def own_gradient(k):
@@ -416,17 +425,15 @@
 
     loop(blocks, finish)
 
-    def give_side(i):
-        j = peer(i)
+    def pack_side(j):
         r.gside[j] = r.sidef[piece_rows(j), :].astype(BF16)
 
-        @pl.when(i > 0)
-        def _():
-            to_group(
-                r.gside.at[j], r.gside_hbm.at[me], r.gside_send.at[0], r.gside_recv.at[0], j
-            ).start()
-
-    loop(groups, give_side)
+    for j in others():
+        pack_side(j)
+        to_group(
+            r.gside.at[j], r.gside_hbm.at[me], r.gside_send.at[0], r.gside_recv.at[0], j
+        ).start()
+    pack_side(me)
     own = pltpu.make_async_copy(r.gside.at[me], r.gside_hbm.at[me], r.gside_own.at[0])
     own.start()
 

time: 212 us -> 177 us (0.83)
  Pallas kernels: 195 us -> 161 us
    pallas_call x1, Pallas kernels: 195 us -> 161 us  [on_device(): pl.pallas_call(partial(kernel, (groups, slices, piece, heads, size), name...]
where the time goes in v2:
time: 177 us
  Pallas kernels  161 us (91%)
  local copies, waits for them, and re-layouts  14 us (8%)
  other arithmetic  2.04 us (1%)
    pallas_call x1, Pallas kernels, on_device(): pl.pallas_call(partial(kernel, (groups, slices, piece, heads, size), name...  161 us
    unnamed x6, local copies, waits for them, and re-layouts  9.14 us

profile of v2, /device:TPU:1, one launch (start us, length us, event | category | flops | bytes accessed | tf_op | source)
XLA Modules:
  0.0 177.2 jit_solution(1805635624787690327)
XLA Ops:
  0.6 0.7 pad.4
  1.3 0.1 pad.7.clone
  1.4 0.6 broadcast_in_dim.19.refs_3_
  2.0 2.0 %maximum_bitcast_fusion.refs_1_ = bf16[32,24,384]{2,1,0:T(8,128)(2,1)} fusion(bf16[1,1,32,24,64]{4,3,2,1,0:T(8,128)(2,1)} %param.9, bf16[1,1,32,24,256]{4,3,2,1,0:T(8,128)(2,1)} %param.8, bf16[384]{0:T(512)(128)(2,1)S(1)} %pad.7.clone), kind=kLoop, calls=%fused_computation | loop fusion | flops 1769472 | bytes 1082112 | tf_op jit(solution)/shard_map/reshape | solution.py:467
  4.0 160.5 %layer.1 = (bf16[768,4096]{1,0:T(8,128)(2,1)}, bf16[32,24,4096]{2,1,0:T(8,128)(2,1)}, bf16[32,24,384]{2,1,0:T(8,128)(2,1)}) custom-call(bf16[32,24,4096]{2,1,0:T(8,128)(2,1)} %bitcast.7, bf16[32,24,384]{2,1,0:T(8,128)(2,1)} %maximum_bitcast_fusion.refs_1_, bf16[768,4096]{1,0:T(8,128)(2,1)} %bitcast.8, f32[8,128]{1,0:T(8,128)} %broadcast_in_dim.19.refs_3_, ...), custom_call_target="tpu_custom_call" | custom-call | tf_op jit(solution)/shard_map/layer/pallas_call | solution.py:527
  164.5 1.6 slice.9
  166.2 0.0 slice-start
  166.2 1.9 %slice.8 = bf16[1,1,32,24,256]{4,3,2,1,0:T(8,128)(2,1)} slice(bf16[1,1,32,24,384]{4,3,2,1,0:T(8,128)(2,1)} %bitcast.14), slice={[0:1], [0:1], [0:32], [0:24], [0:256]} | slice | bytes 786432 | tf_op jit(solution)/shard_map/slice | solution.py:548
  168.1 0.0 slice-start.1
  168.1 6.4 %copy.13 = bf16[1,768,4096]{2,1,0:T(8,128)(2,1)} copy(bf16[1,768,4096]{2,1,0:T(8,128)(2,1)} %bitcast.12) | data formatting | bytes 12582912
  174.5 0.0 slice-done
  174.5 0.0 slice-done.1
  174.5 2.7 %copy.14 = bf16[1,1,32,24,4096]{4,3,2,1,0:T(8,128)(2,1)} copy(bf16[1,1,32,24,4096]{4,3,2,1,0:T(8,128)(2,1)S(1)} %bitcast.11) | data formatting | bytes 12582912
  (2 shorter events, 0.0 us)
Async XLA Ops:
  166.2 8.4 %slice-start = ((s8[6291456]{0:T(1024)(128)(4,1)}), s8[4194304]{0:T(1024)(128)(4,1)S(1)}, s32[]{:S(2)}) async-start(s8[6291456]{0:T(1024)(128)(4,1)} %bitcast.9), calls=%async_computation | async-start | bytes 8388608
  168.1 6.4 %slice-start.1 = ((s8[6291456]{0:T(1024)(128)(4,1)}), s8[2097152]{0:T(1024)(128)(4,1)S(1)}, s32[]{:S(2)}) async-start(s8[6291456]{0:T(1024)(128)(4,1)} %bitcast.9), calls=%async_computation.1 | async-start | bytes 4194304

commit v3 on v2

--- a/solution.py
+++ b/solution.py
@@ -114,11 +114,19 @@
     loop(slices - 1, greet_context)
     pl.semaphore_wait(barrier, groups + slices - 2)
 
+    side_refs = ((r.maps_hbm, r.maps), (r.steps_hbm, r.steps))
+
     def send_side(j):
-        to_group(r.side_hbm.at[j], r.side.at[me], r.side_send.at[0], r.side_recv.at[0], j).start()
+        for n, (source, target) in enumerate(side_refs):
+            to_group(
+                source.at[j], target.at[me], r.side_send.at[n], r.side_recv.at[n], j
+            ).start()
 
     def own_side():
-        return pltpu.make_async_copy(r.side_hbm.at[me], r.side.at[me], r.side_own.at[0])
+        return [
+            pltpu.make_async_copy(source.at[me], target.at[me], r.side_own.at[n])
+            for n, (source, target) in enumerate(side_refs)
+        ]
 
     def send_values(k):
         for j in others():
@@ -142,15 +150,21 @@
 
     for j in others():
         send_side(j)
-    own_side().start()
+    for copy in own_side():
+        copy.start()
     loop(min(AHEAD, chunks), send_values)
     load_grad(0).start()
 
-    take(r.side.at[pl.ds(0, groups - 1)], r.side_recv.at[0])
-    own_side().wait()
+    for n, (_, target) in enumerate(side_refs):
+        take(target.at[pl.ds(0, groups - 1)], r.side_recv.at[n])
+    for copy in own_side():
+        copy.wait()
+    step_at = slice(2 * LANES, 2 * LANES + heads)
+    r.sidef[:, 2 * LANES :] = jnp.zeros((seq, LANES), F32)
 
     def unpack_side(j):
-        r.sidef[piece_rows(j), :] = r.side[j].astype(F32)
+        r.sidef[piece_rows(j), : 2 * LANES] = r.maps[j].astype(F32)
+        r.sidef[piece_rows(j), step_at] = r.steps[j].astype(F32)
 
     loop(groups, unpack_side)
 
@@ -163,7 +177,9 @@
 
     row_at = lax.broadcasted_iota(jnp.int32, (BLOCK, BLOCK), 0)
     col_at = lax.broadcasted_iota(jnp.int32, (BLOCK, BLOCK), 1)
-    rate = r.rate[0:1, :]
+    rate = r.rate[...]
+    if heads < LANES:
+        rate = jnp.concatenate([rate, jnp.zeros((1, LANES - heads), F32)], axis=1)
 
     def block_segments(b):
         first = offset + b * BLOCK
@@ -425,17 +441,25 @@
 
     loop(blocks, finish)
 
+    gside_refs = ((r.gmaps, r.gmaps_hbm), (r.gsteps, r.gsteps_hbm))
+
     def pack_side(j):
-        r.gside[j] = r.sidef[piece_rows(j), :].astype(BF16)
+        r.gmaps[j] = r.sidef[piece_rows(j), : 2 * LANES].astype(BF16)
+        r.gsteps[j] = r.sidef[piece_rows(j), step_at].astype(BF16)
 
     for j in others():
         pack_side(j)
-        to_group(
-            r.gside.at[j], r.gside_hbm.at[me], r.gside_send.at[0], r.gside_recv.at[0], j
-        ).start()
+        for n, (source, target) in enumerate(gside_refs):
+            to_group(
+                source.at[j], target.at[me], r.gside_send.at[n], r.gside_recv.at[n], j
+            ).start()
     pack_side(me)
-    own = pltpu.make_async_copy(r.gside.at[me], r.gside_hbm.at[me], r.gside_own.at[0])
-    own.start()
+    own = [
+        pltpu.make_async_copy(source.at[me], target.at[me], r.gside_own.at[n])
+        for n, (source, target) in enumerate(gside_refs)
+    ]
+    for copy in own:
+        copy.start()
 
     def settle(k):
         take(r.vals.at[k, pl.ds(0, groups - 1)], r.val_send.at[k])
@@ -447,9 +471,29 @@
     loop(chunks, settle)
     for k in range(max(chunks - 2, 0), chunks):
         store_out(k).wait()
-    own.wait()
+    for copy in own:
+        copy.wait()
     for sem in (r.side_send, r.gside_send, r.gside_recv):
-        take(r.side.at[pl.ds(0, groups - 1)], sem.at[0])
+        for n, (_, like) in enumerate(side_refs):
+            take(like.at[pl.ds(0, groups - 1)], sem.at[n])
+
+
+COPY_PARTS = 8
+
+
+def hand_over(*refs):
+    count = len(refs) // 2
+    sems = refs[-1]
+    copies = []
+    for n, (source, target) in enumerate(zip(refs[:count], refs[count : 2 * count])):
+        length = source.shape[0] // COPY_PARTS
+        for p in range(COPY_PARTS):
+            at = pl.ds(p * length, length)
+            copies.append(pltpu.make_async_copy(source.at[at], target.at[at], sems.at[n, p]))
+    for copy in copies:
+        copy.start()
+    for copy in copies:
+        copy.wait()
 
 
 def on_device(inputs_load, maps_load, steps_load, decay_rate, doc_lengths, forget_flags, out_grad):
@@ -461,19 +505,16 @@
     blocks = seq // BLOCK
     chunks = heads // CHUNK_HEADS
     width = CHUNK_HEADS * size
-    fill = LANES - heads
-    side = jnp.concatenate(
-        [maps_load, steps_load, jnp.zeros(steps_load.shape[:-1] + (fill,), BF16)], axis=-1
-    ).reshape(groups, piece, 3 * LANES)
-    rate = jnp.broadcast_to(jnp.pad(decay_rate, (0, fill))[None], (8, LANES))
 
     dma = pltpu.SemaphoreType.DMA
     vmem = pltpu.VMEM
     scratch = dict(
         vals=vmem((chunks, groups, piece, width), BF16),
         gsend=vmem((chunks, groups, piece, width), BF16),
-        side=vmem((groups, piece, 3 * LANES), BF16),
-        gside=vmem((groups, piece, 3 * LANES), BF16),
+        maps=vmem((groups, piece, 2 * LANES), BF16),
+        steps=vmem((groups, piece, heads), BF16),
+        gmaps=vmem((groups, piece, 2 * LANES), BF16),
+        gsteps=vmem((groups, piece, heads), BF16),
         sidef=vmem((seq, 3 * LANES), F32),
         og=vmem((3, seq, width), BF16),
         y=vmem((2, seq, width), BF16),
@@ -510,8 +551,8 @@
         db=vmem((blocks, BLOCK, LANES), F32),
         edge=vmem((blocks, BLOCK, LANES), F32),
         dstep=vmem((blocks, BLOCK, LANES), F32),
-        side_send=dma((1,)), side_recv=dma((1,)), side_own=dma((1,)),
-        gside_send=dma((1,)), gside_recv=dma((1,)), gside_own=dma((1,)),
+        side_send=dma((2,)), side_recv=dma((2,)), side_own=dma((2,)),
+        gside_send=dma((2,)), gside_recv=dma((2,)), gside_own=dma((2,)),
         decay_send=dma((1,)), decay_recv=dma((1,)),
         val_send=dma((chunks,)), val_recv=dma((chunks,)), val_own=dma((chunks,)),
         gx_send=dma((chunks,)), gx_recv=dma((chunks,)), gx_own=dma((chunks,)),
@@ -519,35 +560,49 @@
         og_sem=dma((3,)), y_sem=dma((2,)),
     )
     names = (
-        "x_hbm", "side_hbm", "og_hbm", "rate", "lens", "flags", "y_hbm", "gx_hbm", "gside_hbm",
+        "x_hbm", "maps_hbm", "steps_hbm", "og_hbm", "rate", "lens", "flags",
+        "y_hbm", "gx_hbm", "gmaps_hbm", "gsteps_hbm",
     ) + tuple(scratch)
     anywhere = pl.BlockSpec(memory_space=pl.ANY)
     in_vmem = pl.BlockSpec(memory_space=pltpu.VMEM)
     in_smem = pl.BlockSpec(memory_space=pltpu.SMEM)
-    y, gx, gside = pl.pallas_call(
+    y, gx, gmaps, gsteps = pl.pallas_call(
         partial(kernel, (groups, slices, piece, heads, size), names),
         out_shape=(
-            jax.ShapeDtypeStruct((seq, total), BF16),
-            jax.ShapeDtypeStruct((groups, piece, total), BF16),
-            jax.ShapeDtypeStruct((groups, piece, 3 * LANES), BF16),
+            pltpu.VMEM((seq, total), BF16),
+            pltpu.VMEM((groups, piece, total), BF16),
+            pltpu.VMEM((groups, piece, 2 * LANES), BF16),
+            pltpu.VMEM((groups, piece, heads), BF16),
         ),
-        in_specs=[anywhere, anywhere, anywhere, in_vmem, in_smem, in_smem],
-        out_specs=[anywhere, anywhere, anywhere],
+        in_specs=[anywhere] * 4 + [in_vmem, in_smem, in_smem],
+        out_specs=[anywhere] * 4,
         scratch_shapes=list(scratch.values()),
         compiler_params=pltpu.CompilerParams(
-            collective_id=0, has_side_effects=True, vmem_limit_bytes=60 * 1024 * 1024
+            collective_id=0, has_side_effects=True, vmem_limit_bytes=47 * 1024 * 1024
         ),
         name="layer",
     )(
-        inputs_load.reshape(groups, piece, total), side, out_grad[0], rate, doc_lengths, forget_flags
+        inputs_load[0, 0],
+        maps_load[0, 0],
+        steps_load[0, 0],
+        out_grad[0],
+        decay_rate[None],
+        doc_lengths,
+        forget_flags,
     )
-    gside = gside[None, None]
-    return (
-        y[None],
-        gx[None, None],
-        gside[..., : 2 * LANES],
-        gside[..., 2 * LANES : 2 * LANES + heads],
+    held = tuple(
+        pltpu.with_memory_space_constraint(a, pltpu.VMEM) for a in (y, gx, gmaps, gsteps)
     )
+    y, gx, gmaps, gsteps = pl.pallas_call(
+        hand_over,
+        out_shape=tuple(jax.ShapeDtypeStruct(a.shape, a.dtype) for a in held),
+        in_specs=[anywhere] * 4,
+        out_specs=[anywhere] * 4,
+        scratch_shapes=[dma((4, COPY_PARTS))],
+        compiler_params=pltpu.CompilerParams(vmem_limit_bytes=1024 * 1024),
+        name="hand_over",
+    )(*held)
+    return y[None], gx[None, None], gmaps[None, None], gsteps[None, None]
 
 
 def solution(mesh):

time: 177 us -> 166 us (0.938)
  local copies, waits for them, and re-layouts: 14 us -> 0 us
  Pallas kernels: 161 us -> 166 us
  other arithmetic: 2.04 us -> 0 us
    unnamed x6 -> x0, local copies, waits for them, and re-layouts: 9.14 us -> none
    pallas_call x0 -> x1, Pallas kernels: none -> 4.98 us  [on_device(): pl.pallas_call(hand_over, out_shape=tuple((jax.ShapeDtypeStruct(a.shape,...]
    slice x2 -> x0, local copies, waits for them, and re-layouts: 3.54 us -> none  [the longest x1 1.92 us: on_device(): gside[..., :2 * LANES]]
    reshape x1 -> x0, other arithmetic: 2.04 us -> none  [on_device(): side = jnp.concatenate([maps_load, steps_load, jnp.zeros(steps_load.shape...]
where the time goes in v3:
time: 166 us
  Pallas kernels  166 us (100%)
    pallas_call x1, Pallas kernels, on_device(): pl.pallas_call(partial(kernel, (groups, slices, piece, heads, size), name...  161 us
    pallas_call x1, Pallas kernels, on_device(): pl.pallas_call(hand_over, out_shape=tuple((jax.ShapeDtypeStruct(a.shape,...  4.98 us

profile of v3, /device:TPU:1, one launch (start us, length us, event | category | flops | bytes accessed | tf_op | source)
XLA Modules:
  0.0 166.2 jit_solution(16192271975999169044)
XLA Ops:
  0.6 160.5 %layer.1 = (bf16[768,4096]{1,0:T(8,128)(2,1)S(1)}, bf16[32,24,4096]{2,1,0:T(8,128)(2,1)S(1)}, bf16[32,24,256]{2,1,0:T(8,128)(2,1)S(1)}, bf16[32,24,64]{2,1,0:T(8,128)(2,1)S(1)}) custom-call(bf16[32,24,4096]{2,1,0:T(8,128)(2,1)} %bitcast.9, bf16[32,24,256]{2,1,0:T(8,128)(2,1)} %bitcast.11, bf16[32,24,64]{2,1,0:T(8,128)(2,1)} %bitcast.12, ...), custom_call_target="tpu_custom_call" | custom-call | tf_op jit(solution)/shard_map/layer/pallas_call | solution.py:569
  161.2 5.0 %hand_over.1 = (bf16[768,4096]{1,0:T(8,128)(2,1)}, bf16[32,24,4096]{2,1,0:T(8,128)(2,1)}, bf16[32,24,256]{2,1,0:T(8,128)(2,1)}, bf16[32,24,64]{2,1,0:T(8,128)(2,1)}) custom-call(bf16[768,4096]{1,0:T(8,128)(2,1)S(1)} %get-tuple-element.12.refs_0_, bf16[32,24,4096]{2,1,0:T(8,128)(2,1)S(1)} %get-tuple-element.13.refs_1_, ...), custom_call_target="tpu_custom_call" | custom-call | tf_op jit(solution)/shard_map/hand_over/pallas_call | solution.py:596

commit v4 on v3

--- a/solution.py
+++ b/solution.py
@@ -486,8 +486,9 @@
     sems = refs[-1]
     copies = []
     for n, (source, target) in enumerate(zip(refs[:count], refs[count : 2 * count])):
-        length = source.shape[0] // COPY_PARTS
-        for p in range(COPY_PARTS):
+        parts = COPY_PARTS if source.shape[-1] > 2 * LANES else 1
+        length = source.shape[0] // parts
+        for p in range(parts):
             at = pl.ds(p * length, length)
             copies.append(pltpu.make_async_copy(source.at[at], target.at[at], sems.at[n, p]))
     for copy in copies:

time: 166 us -> 166 us (level)
  no operation moved by 1% of the time
where the time goes in v4:
time: 166 us
  Pallas kernels  166 us (100%)
    pallas_call x1, Pallas kernels, on_device(): pl.pallas_call(partial(kernel, (groups, slices, piece, heads, size), name...  161 us
    pallas_call x1, Pallas kernels, on_device(): pl.pallas_call(hand_over, out_shape=tuple((jax.ShapeDtypeStruct(a.shape,...  5 us

profile of v4, /device:TPU:1, one launch (start us, length us, event | category | flops | bytes accessed | tf_op | source)
XLA Modules:
  0.0 166.2 jit_solution(11359392721352006821)
XLA Ops:
  0.6 160.5 %layer.1 = (bf16[768,4096]{1,0:T(8,128)(2,1)S(1)}, bf16[32,24,4096]{2,1,0:T(8,128)(2,1)S(1)}, bf16[32,24,256]{2,1,0:T(8,128)(2,1)S(1)}, bf16[32,24,64]{2,1,0:T(8,128)(2,1)S(1)}) custom-call(bf16[32,24,4096]{2,1,0:T(8,128)(2,1)} %bitcast.9, bf16[32,24,256]{2,1,0:T(8,128)(2,1)} %bitcast.11, bf16[32,24,64]{2,1,0:T(8,128)(2,1)} %bitcast.12, ...), custom_call_target="tpu_custom_call" | custom-call | tf_op jit(solution)/shard_map/layer/pallas_call | solution.py:570
  161.2 5.0 %hand_over.1 = (bf16[768,4096]{1,0:T(8,128)(2,1)}, bf16[32,24,4096]{2,1,0:T(8,128)(2,1)}, bf16[32,24,256]{2,1,0:T(8,128)(2,1)}, bf16[32,24,64]{2,1,0:T(8,128)(2,1)}) custom-call(bf16[768,4096]{1,0:T(8,128)(2,1)S(1)} %get-tuple-element.12.refs_0_, bf16[32,24,4096]{2,1,0:T(8,128)(2,1)S(1)} %get-tuple-element.13.refs_1_, ...), custom_call_target="tpu_custom_call" | custom-call | tf_op jit(solution)/shard_map/hand_over/pallas_call | solution.py:597
